TPU v7x, 128 devices: a whole 4x4x4 slice. The times are simulated.
128 devices in a mesh: dp: 8 (over z, core), space: 16 (over x, y).
Axes of the slice: x: 4, y: 4, z: 4, core: 2. Of those that a mesh axis runs over, the one named last changes fastest.
Arguments:
- feats: bfloat16 [16, 128, 128, 1536], P('dp', 'space'), may hold values from -6 to 6
- lateral: bfloat16 [1536, 512], replicated, may hold values from -0.15625 to 0.15625
- kernel: float32 [7, 7, 512], replicated, may hold values from -0.875 to 0.875
- grad_out: bfloat16 [16, 128, 128, 512], P('dp', 'space'), may hold values from -6 to 6
- error: float32 [196608, 512], P(('dp', 'space')), may hold values from -192 to 192
- q_prev: float32 [512, 8], replicated, may hold values from -6 to 6
Outputs:
- smoothed: bfloat16 [16, 128, 128, 512], P('dp', 'space')
- grad_feats: bfloat16 [16, 128, 128, 1536], P('dp', 'space')
- q_next: float32 [512, 8], replicated
- update: float32 [1536, 512], P('space')
- error_next: float32 [196608, 512], P(('dp', 'space'))
All inputs are finite; a program needn't handle non-finite values.
Results may differ from a plain program's by a relative error of at most 0.0049.
Values may be sent and summed in bfloat16 or wider, within the bound.
A program may use at most 128 MiB of HBM per device.

v0:
```python
import jax
import jax.numpy as jnp
from jax import lax
from jax.sharding import PartitionSpec as P


def extended(block, sides, width):
    for axis, dim in sides:
        count = lax.axis_size(axis)
        forward = [(i, i + 1) for i in range(count - 1)]
        backward = [(target, source) for source, target in forward]
        low = lax.ppermute(
            lax.slice_in_dim(block, block.shape[dim] - width, None, axis=dim), axis, forward
        )
        high = lax.ppermute(lax.slice_in_dim(block, 0, width, axis=dim), axis, backward)
        block = jnp.concatenate([low, block, high], axis=dim)
    return block


def depthwise(padded, kernel, rows, cols, flip):
    size = kernel.shape[0]
    total = jnp.zeros(padded.shape[:1] + (rows, cols, padded.shape[3]), jnp.float32)
    for a in range(size):
        for c in range(size):
            if flip:
                top, left = (size - 1 - a, size - 1 - c)
            else:
                top, left = (a, c)
            piece = padded[:, top : top + rows, left : left + cols, :].astype(jnp.float32)
            total = total + kernel[a, c] * piece
    return total


def orthonormal(matrix):
    finished = []
    for index in range(matrix.shape[1]):
        column = matrix[:, index]
        for other in finished:
            column = column - jnp.sum(other * column) * other
        column = column / jnp.sqrt(jnp.sum(column * column) + 1e-06)
        finished.append(column)
    return jnp.stack(finished, axis=1)


def combine_columns(local_left):
    return lax.psum(local_left, ("dp", "space"))


def combine_rows(local_right):
    return lax.psum(local_right, ("dp", "space"))


def body(feats, lateral, kernel, grad_out, error, q_prev):
    size = kernel.shape[0]
    half = size // 2
    highest = lax.Precision.HIGHEST
    tiles, rows, cols, channels = feats.shape
    width_out = lateral.shape[1]
    count = lax.axis_size("dp") * lax.axis_size("space")
    flat = feats.reshape(-1, channels)
    column_pad = ((0, 0), (0, 0), (half, half), (0, 0))
    grad_rims = extended(grad_out, (("space", 1),), half)
    projected = jnp.dot(flat, lateral, preferred_element_type=jnp.float32).astype(jnp.bfloat16)
    projected = projected.reshape(tiles, rows, cols, width_out)
    proj_rims = extended(projected, (("space", 1),), half)
    smoothed = depthwise(jnp.pad(proj_rims, column_pad), kernel, rows, cols, False).astype(
        jnp.bfloat16
    )
    grad_proj = depthwise(jnp.pad(grad_rims, column_pad), kernel, rows, cols, True).astype(
        jnp.bfloat16
    )
    grad_flat = grad_proj.reshape(-1, width_out)
    grad_feats = jnp.dot(grad_flat, lateral.T, preferred_element_type=jnp.float32)
    grad_feats = grad_feats.astype(jnp.bfloat16).reshape(tiles, rows, cols, channels)
    contract = (((0,), (0,)), ((), ()))
    gradient = lax.dot_general(flat, grad_flat, contract, preferred_element_type=jnp.float32)
    matrix = gradient + error
    local_left = jnp.dot(matrix, q_prev, precision=highest)
    left = combine_columns(local_left) / count
    basis = orthonormal(left)
    local_right = lax.dot_general(
        matrix, basis, contract, precision=highest, preferred_element_type=jnp.float32
    )
    q_next = combine_rows(local_right) / count
    full_update = jnp.dot(basis, q_next.T, precision=highest)
    error_next = matrix - full_update
    share = channels // lax.axis_size("space")
    update = lax.dynamic_slice_in_dim(full_update, lax.axis_index("space") * share, share, 0)
    return (smoothed, grad_feats, q_next, update, error_next)


def solution(mesh):
    placed = (
        P("dp", "space", None, None),
        P(),
        P(),
        P("dp", "space", None, None),
        P(("dp", "space"), None),
        P(),
    )
    return jax.shard_map(
        body,
        mesh=mesh,
        in_specs=placed,
        out_specs=(
            P("dp", "space", None, None),
            P("dp", "space", None, None),
            P(),
            P("space", None),
            P(("dp", "space"), None),
        ),
        check_vma=False,
    )
```

profile of v0, /device:TPU:1, one launch (start us, length us, event | category | flops | bytes accessed | tf_op | source)
XLA Modules:
  0.0 371.9 jit_solution(6870809358475370287)
XLA Ops:
  0.6 2.8 fusion.8
  3.4 4.9 %collective-permute-start.2 = (bf16[2,3,128,512]{3,2,1,0:T(8,128)(2,1)}, bf16[2,3,128,512]{3,2,1,0:T(8,128)(2,1)}, u32[]{:S(2)}, u32[]{:S(2)}) collective-permute-start(bf16[2,3,128,512]{3,2,1,0:T(8,128)(2,1)} %get-tuple-element.75), channel_id=1, source_target_pairs={{0,1},{1,2},{2,3},{3,4},{4,5},{5,6},{6,7},{7,8},{8,9},{9,10},{10,1... | collective-permute-start | bytes 2359304 | tf_op jit(solution)/shard_map/ppermute | solution.py:12
  9.6 6.4 %convolution_convert_fusion.1 = bf16[2048,512]{1,0:T(8,128)(2,1)S(1)} fusion(bf16[2048,1536]{1,0:T(8,128)(2,1)} %bitcast.77, bf16[1536,512]{1,0:T(8,128)(2,1)S(1)} %copy-done), kind=kOutput, calls=%fused_computation.17 | convolution fusion | flops 3222274048 | bytes 9961472 | tf_op jit(solution)/shard_map/dot_general | solution.py:63
  18.8 4.0 %collective-permute-start = (bf16[2,3,128,512]{3,2,1,0:T(8,128)(2,1)}, bf16[2,3,128,512]{3,2,1,0:T(8,128)(2,1)S(1)}, u32[]{:S(2)}, u32[]{:S(2)}) collective-permute-start(bf16[2,3,128,512]{3,2,1,0:T(8,128)(2,1)} %get-tuple-element.77), channel_id=1, source_target_pairs={{0,1},{1,2},{2,3},{3,4},{4,5},{5,6},{6,7},{7,8},{8,9},{9,10},{10,1... | collective-permute-start | bytes 2359304 | tf_op jit(solution)/shard_map/ppermute | solution.py:12
  24.1 3.5 copy.12
  29.1 3.3 constant_dynamic-update-slice_fusion.1
  32.4 4.7 %select_maximum_fusion = bf16[2,14,134,512]{3,2,1,0:T(8,128)(2,1)} fusion(bf16[2,3,128,512]{3,2,1,0:T(8,128)(2,1)} %collective-permute-done.3, bf16[2,8,128,512]{3,2,1,0:T(8,128)(2,1)S(1)} %copy-done.2, bf16[2,3,128,512]{3,2,1,0:T(8,128)(2,1)} %collective-permute-done.2), kind=kLoop, calls=%fused_computation.6 | loop fusion | flops 23052288 | bytes 7512064 | tf_op jit(solution)/shard_map/concatenate | solution.py:16
  37.0 2.1 constant_dynamic-update-slice_fusion
  39.2 61.2 %add_convert_fusion = bf16[2,8,128,512]{3,2,1,0:T(8,128)(2,1)} fusion(bf16[2,8,128,512]{3,2,1,0:T(8,128)(2,1)} %param.9, bf16[2,14,134,512]{3,2,1,0:T(8,128)(2,1)} %select_maximum_fusion, bf16[2,11,128,512]{3,2,1,0:T(8,128)(2,1)} %copy-done.3, bf16[2,11,128,512]{3,2,1,0:T(8,128)(2,1)} %constant_dynamic-update-slice_fusion, f32[512]{0:T(512)S(1)} %bitcast.134, ...), kind=kLoop, calls=%fused_computation.4 | loop fusion | flops 154140672 | bytes 104957952 | tf_op jit(solution)/shard_map/convert_element_type | solution.py:69
  100.4 7.8 %fusion.2 = f32[1536,512]{0,1:T(8,128)S(1)} fusion(f32[1536,512]{0,1:T(8,128)} %copy.12, bf16[2,8,128,512]{3,2,1,0:T(8,128)(2,1)} %add_convert_fusion, bf16[2,8,128,1536]{3,2,1,0:T(8,128)(2,1)} %param.6), kind=kOutput, calls=%fused_computation.16 | convolution fusion | flops 3222011904 | bytes 14680064 | tf_op jit(solution)/shard_map/dot_general | solution.py:76
  111.6 71.3 %psum.14 = f32[1536,8]{0,1:T(8,128)S(1)} all-reduce(f32[1536,8]{0,1:T(8,128)S(1)} %fusion.13), channel_id=1, replica_groups=mesh['dp'=8,'space'=16] {'dp','space'}, use_global_device_ids=true, to_apply=%region_0.1 | all-reduce | flops 12288 | bytes 98304 | tf_op jit(solution)/shard_map/psum | solution.py:46
  186.9 5.1 %multiply_reduce_fusion.6 = (f32[]{:T(128)}, f32[]{:T(128)}, f32[]{:T(128)}, f32[]{:T(128)}, f32[]{:T(128)}, /*index=5*/f32[]{:T(128)}, f32[1536]{0:T(1024)S(1)}) fusion(f32[1536]{0:T(1024)S(1)} %get-tuple-element.10, f32[1536]{0:T(1024)S(1)} %get-tuple-element.71, f32[]{:T(128)} %get-tuple-element.38, f32[1536]{0:T(1024)S(1)} %get-tuple-element.11, ...), kind=kLoop, calls=%fused_computation.45 | loop fusion | flops 41466 | bytes 55352 | tf_op jit(solution)/shard_map/reduce_sum | solution.py:39
  192.1 2.0 multiply_reduce_fusion.30
  194.7 1.8 multiply_reduce_fusion.27
  196.6 6.3 %multiply_reduce_fusion.5 = (f32[]{:T(128)}, f32[]{:T(128)}, f32[]{:T(128)}, f32[]{:T(128)}, f32[]{:T(128)}, /*index=5*/f32[1536]{0:T(1024)S(1)}, f32[1536]{0:T(1024)S(1)}, f32[1536]{0:T(1024)S(1)}, f32[1536]{0:T(1024)S(1)}) fusion(f32[1536]{0:T(1024)S(1)} %get-tuple-element.69, f32[]{:T(128)S(6)} %sqrt.26, f32[1536]{0:T(1024)S(1)} %get-tuple-element.67, ...), kind=kLoop, calls=%fused_computation.43 | loop fusion | flops 44539 | bytes 73788 | tf_op jit(solution)/shard_map/reduce_sum | solution.py:39
  203.6 3.7 %multiply_reduce_fusion.4 = (f32[]{:T(128)}, f32[]{:T(128)}, f32[]{:T(128)}, f32[]{:T(128)}) fusion(f32[1536]{0:T(1024)S(1)} %get-tuple-element.65, f32[]{:T(128)} %get-tuple-element.33, f32[1536]{0:T(1024)S(1)} %get-tuple-element.69, f32[]{:T(128)S(6)} %sqrt.26, f32[]{:T(128)S(6)} %sqrt.27, f32[1536]{0:T(1024)S(1)} %get-tuple-element.67, ...), kind=kLoop, calls=%fused_computation.41 | loop fusion | flops 30716 | bytes 36908 | tf_op jit(solution)/shard_map/reduce_sum | solution.py:39
  207.3 2.6 multiply_reduce_fusion.21
  210.6 2.6 multiply_reduce_fusion.16
  213.2 4.4 %multiply_reduce_fusion.3 = (f32[]{:T(128)}, f32[]{:T(128)}, f32[]{:T(128)}, f32[1536]{0:T(1024)S(1)}, f32[1536]{0:T(1024)S(1)}) fusion(f32[1536]{0:T(1024)S(1)} %get-tuple-element.61, f32[]{:T(128)S(6)} %sqrt.28, f32[1536]{0:T(1024)S(1)} %get-tuple-element.59, f32[]{:T(128)} %get-tuple-element.58, f32[]{:T(128)S(6)} %sqrt.27, ...), kind=kLoop, calls=%fused_computation.39 | loop fusion | flops 32253 | bytes 49200 | tf_op jit(solution)/shard_map/reduce_sum | solution.py:39
  218.2 2.6 multiply_reduce_fusion.2
  220.8 2.5 multiply_reduce_fusion.8
  224.0 2.7 multiply_reduce_fusion.1
  228.6 17.6 %subtract_divide_fusion = (f32[1536,1]{0,1:T(1,128)S(1)}, f32[1536,1]{0,1:T(1,128)S(1)}, f32[1536,1]{0,1:T(1,128)S(1)}, f32[1536,1]{0,1:T(1,128)S(1)}, f32[1536,...) fusion(f32[1536,1]{0,1:T(1,128)S(1)} %get-tuple-element.72, f32[1536,8]{0,1:T(8,128)S(1)} %broadcast_multiply_fusion, ...), kind=kLoop, calls=%fused_computation.96 | loop fusion | flops 96768 | bytes 92300 | tf_op jit(solution)/shard_map/div | solution.py:40
  246.3 4.6 %fusion.14 = f32[512,8]{0,1:T(8,128)S(1)} fusion(f32[1536,512]{0,1:T(8,128)} %copy-done.1, f32[1536,8]{0,1:T(8,128)S(1)} %stack.2), kind=kOutput, calls=%fused_computation.126 | convolution fusion | flops 75497472 | bytes 3211264 | tf_op jit(solution)/shard_map/dot_general | solution.py:81
  250.9 63.3 %psum.15 = f32[512,8]{0,1:T(8,128)S(1)} all-reduce(f32[512,8]{0,1:T(8,128)S(1)} %fusion.14), channel_id=1, replica_groups=mesh['dp'=8,'space'=16] {'dp','space'}, use_global_device_ids=true, to_apply=%region_37.38 | all-reduce | flops 4096 | bytes 32768 | tf_op jit(solution)/shard_map/psum | solution.py:50
  314.2 4.3 %fusion.15 = f32[1536,512]{1,0:T(8,128)} fusion(f32[1536,8]{0,1:T(8,128)S(1)} %stack.2, f32[512,8]{0,1:T(8,128)S(1)} %broadcast_multiply_fusion.1), kind=kOutput, calls=%fused_computation.127 | convolution fusion | flops 75497472 | bytes 3211264 | tf_op jit(solution)/shard_map/dot_general | solution.py:85
  318.5 3.5 copy.13
  322.1 5.1 %sub.283 = f32[1536,512]{0,1:T(8,128)} subtract(f32[1536,512]{0,1:T(8,128)} %copy-done.1, f32[1536,512]{0,1:T(8,128)} %copy.13) | non-fusion elementwise | flops 786432 | bytes 9437184 | tf_op jit(solution)/shard_map/sub | solution.py:86
  327.2 3.5 copy.14
  332.3 7.1 %convolution_convert_fusion = bf16[2048,1536]{1,0:T(8,128)(2,1)} fusion(bf16[2048,512]{1,0:T(8,128)(2,1)} %bitcast.76, bf16[1536,512]{1,0:T(8,128)(2,1)S(1)} %copy-done), kind=kOutput, calls=%fused_computation.3 | convolution fusion | flops 3224371200 | bytes 9961472 | tf_op jit(solution)/shard_map/dot_general | solution.py:73
  339.4 1.8 select_maximum_fusion.2
  341.2 30.8 %add_convert_fusion.1 = bf16[2,8,128,512]{3,2,1,0:T(8,128)(2,1)} fusion(bf16[2,8,128,512]{3,2,1,0:T(8,128)(2,1)S(1)} %bitcast.75, bf16[2,3,128,512]{3,2,1,0:T(8,128)(2,1)S(1)} %collective-permute-done.1, bf16[2,3,128,512]{3,2,1,0:T(8,128)(2,1)S(1)} %collective-permute-done, bf16[2,14,134,512]{3,2,1,0:T(8,128)(2,1)S(1)} %select_maximum_fusion.2, ...), kind=kLoop, calls=%fused_computation.5 | loop fusion | flops 160432128 | bytes 93947904 | tf_op jit(solution)/shard_map/convert_element_type | solution.py:66
  (39 shorter events, 15.8 us)
Async XLA Ops:
  0.6 9.0 %copy-start = (bf16[1536,512]{1,0:T(8,128)(2,1)S(1)}, bf16[1536,512]{1,0:T(8,128)(2,1)}, u32[]{:S(2)}) copy-start(bf16[1536,512]{1,0:T(8,128)(2,1)} %param.7) | copy-start | bytes 4718596
  3.4 24.4 %collective-permute-start.2 = (bf16[2,3,128,512]{3,2,1,0:T(8,128)(2,1)}, bf16[2,3,128,512]{3,2,1,0:T(8,128)(2,1)}, u32[]{:S(2)}, u32[]{:S(2)}) collective-permute-start(bf16[2,3,128,512]{3,2,1,0:T(8,128)(2,1)} %get-tuple-element.75), channel_id=1, source_target_pairs={{0,1},{1,2},{2,3},{3,4},{4,5},{5,6},{6,7},{7,8},{8,9},{9,10},{10,1... | collective-permute-start | bytes 2359304 | tf_op jit(solution)/shard_map/ppermute | solution.py:12
  8.3 24.1 %collective-permute-start.3 = (bf16[2,3,128,512]{3,2,1,0:T(8,128)(2,1)}, bf16[2,3,128,512]{3,2,1,0:T(8,128)(2,1)}, u32[]{:S(2)}, u32[]{:S(2)}) collective-permute-start(bf16[2,3,128,512]{3,2,1,0:T(8,128)(2,1)} %get-tuple-element.76), channel_id=1, source_target_pairs={{1,0},{2,1},{3,2},{4,3},{5,4},{6,5},{7,6},{8,7},{9,8},{10,9},{11,1... | collective-permute-start | bytes 2359304 | tf_op jit(solution)/shard_map/ppermute | solution.py:15
  16.1 1.3 copy-start.4
  17.4 10.3 %copy-start.6 = (f32[7,7,512]{2,1,0:T(8,128)S(1)}, f32[7,7,512]{2,1,0:T(8,128)}, u32[]{:S(2)}) copy-start(f32[7,7,512]{2,1,0:T(8,128)} %param.8) | copy-start | bytes 301060
  18.8 320.6 %collective-permute-start = (bf16[2,3,128,512]{3,2,1,0:T(8,128)(2,1)}, bf16[2,3,128,512]{3,2,1,0:T(8,128)(2,1)S(1)}, u32[]{:S(2)}, u32[]{:S(2)}) collective-permute-start(bf16[2,3,128,512]{3,2,1,0:T(8,128)(2,1)} %get-tuple-element.77), channel_id=1, source_target_pairs={{0,1},{1,2},{2,3},{3,4},{4,5},{5,6},{6,7},{7,8},{8,9},{9,10},{10,1... | collective-permute-start | bytes 2359304 | tf_op jit(solution)/shard_map/ppermute | solution.py:12
  22.8 316.6 %collective-permute-start.1 = (bf16[2,3,128,512]{3,2,1,0:T(8,128)(2,1)}, bf16[2,3,128,512]{3,2,1,0:T(8,128)(2,1)S(1)}, u32[]{:S(2)}, u32[]{:S(2)}) collective-permute-start(bf16[2,3,128,512]{3,2,1,0:T(8,128)(2,1)} %get-tuple-element.78), channel_id=1, source_target_pairs={{1,0},{2,1},{3,2},{4,3},{5,4},{6,5},{7,6},{8,7},{9,8},{10,9},{11,1... | collective-permute-start | bytes 2359304 | tf_op jit(solution)/shard_map/ppermute | solution.py:15
  27.7 4.7 %copy-start.2 = (bf16[2,8,128,512]{3,2,1,0:T(8,128)(2,1)S(1)}, bf16[2,8,128,512]{3,2,1,0:T(8,128)(2,1)}, u32[]{:S(2)}) copy-start(bf16[2,8,128,512]{3,2,1,0:T(8,128)(2,1)} %param.9) | copy-start | bytes 6291460
  32.4 6.8 %copy-start.3 = (bf16[2,11,128,512]{3,2,1,0:T(8,128)(2,1)}, bf16[2,11,128,512]{3,2,1,0:T(8,128)(2,1)S(1)}, u32[]{:S(2)}) copy-start(bf16[2,11,128,512]{3,2,1,0:T(8,128)(2,1)S(1)} %get-tuple-element.74) | copy-start | bytes 8650756
  100.4 9.5 %copy-start.8 = (f32[512,8]{0,1:T(8,128)S(1)}, f32[512,8]{0,1:T(8,128)}, u32[]{:S(2)}) copy-start(f32[512,8]{0,1:T(8,128)} %param.11) | copy-start | bytes 49156
  108.2 1.7 copy-start.1
  314.2 7.9 %copy-start.7 = (f32[512,8]{0,1:T(8,128)}, f32[512,8]{0,1:T(8,128)S(1)}, u32[]{:S(2)}) copy-start(f32[512,8]{0,1:T(8,128)S(1)} %broadcast_multiply_fusion.1) | copy-start | bytes 49156
  332.3 7.1 %copy-start.5 = (bf16[2048,512]{1,0:T(8,128)(2,1)S(1)}, bf16[2048,512]{1,0:T(8,128)(2,1)}, u32[]{:S(2)}) copy-start(bf16[2048,512]{1,0:T(8,128)(2,1)} %copy-done.4) | copy-start | bytes 6291460
where the time goes:
time: 373 us; the launch traced here: 372 us
  other arithmetic  161 us (43%)
  blocking collectives  135 us (36%)
  matrix products  31.9 us (9%)
  local copies, waits for them, and re-layouts  26.3 us (7%)
  starting transfers between devices  11.5 us (3%)
  between operations  6.24 us (2%)
    psum x1, blocking collectives, combine_columns(): return lax.psum(local_left, ('dp', 'space'))  71.3 us
    psum x1, blocking collectives, combine_rows(): return lax.psum(local_right, ('dp', 'space'))  63.3 us
    convert_element_type x1, other arithmetic, body(): depthwise(jnp.pad(grad_rims, column_pad), kernel, rows, cols, True)  61.2 us
    reduce_sum x10, other arithmetic, orthonormal(): column = column - jnp.sum(other * column) * other  31.2 us
    convert_element_type x1, other arithmetic, body(): depthwise(jnp.pad(proj_rims, column_pad), kernel, rows, cols, False)  30.8 us
    div x2, other arithmetic, orthonormal(): column = column / jnp.sqrt(jnp.sum(column * column) + 1e-06)  17.6 us
    unnamed x22, local copies, waits for them, and re-layouts  14.7 us
    ppermute x2, starting transfers between devices, extended(): lax.ppermute(lax.slice_in_dim(block, block.shape[dim] - width, None, axis...  8.94 us
  transfers between devices with their start and end apart: 4, of which 0 were waited for; matrix products, arithmetic and copies ran while one was open for 49% of the time, Pallas kernels for 0%

commit v1 on v0

v1 whole, which is shorter than its diff:
```python
import jax
import jax.numpy as jnp
from jax import lax
from jax.experimental import pallas as pl
from jax.experimental.pallas import tpu as pltpu
from jax.sharding import PartitionSpec as P

MESH = pl.DeviceIdType.MESH
BF = jnp.bfloat16
F32 = jnp.float32
TAPS = 7
HALF = 3
LEAVES = 26
SEG = 16
SEGS = 8
EXT = (SEG + 2 * HALF) * SEGS
PIECES = 8
WINDOW = 3


def leaf_inputs(d):
    if len(d) == 1:
        return [d[0]]
    size = (len(d) + 1) // 2
    half, span = size // 2, size - 1
    sub = lambda x, y: None if x is None or y is None else x - y
    d0, d1, d2 = d[:span], d[half : half + span], d[size : size + span]
    first = [sub(x, y) for x, y in zip(d0, d1)]
    last = [sub(x, y) for x, y in zip(d2, d1)]
    return leaf_inputs(first) + leaf_inputs(d1) + leaf_inputs(last)


def leaf_weights(h):
    if len(h) == 1:
        return [h[0]]
    half = len(h) // 2
    low, high = h[:half], h[half:]
    both = [x if y is None else x + y for x, y in zip(low, high)]
    return leaf_weights(low) + leaf_weights(both) + leaf_weights(high)


def leaf_outputs(m):
    if len(m) == 1:
        return [m[0]]
    third = len(m) // 3
    first, mid, last = (leaf_outputs(m[i * third : (i + 1) * third]) for i in range(3))
    add = lambda x, y: x if y is None else x + y
    return [add(y, x) for x, y in zip(first, mid)] + [add(x, y) for x, y in zip(mid, last)]


def split(x):
    high = x.astype(BF)
    return high, (x - high.astype(F32)).astype(BF)


def stacked(x):
    high = x.astype(BF).astype(F32)
    return jnp.concatenate([high, x - high], axis=0).astype(BF)


def nt(x, y):
    return lax.dot_general(x, y, (((1,), (1,)), ((), ())), preferred_element_type=F32)


def fold(x):
    return x[:8] + x[8:16]


def main_kernel(
    feats_h, lateral_h, grad_h, error_h, kernel_ref, q_ref,
    gp_h, sm_h, basis_ref, qt_ref,
    feats, lateral, grad, error, proj, gp, sm,
    halo_g, halo_p, own_g, own_p, rims, leaf_u, leaf_v, weights, pieces,
    p_buf, p_rs, p_part, p_all, p_out, r_buf, r_rs, r_part, r_all, r_out,
    in_sem, feats_sem, out_sem, halo_send, halo_recv, send1, recv1, send2, recv2, send3, recv3,
):
    s, d = lax.axis_index("space"), lax.axis_index("dp")
    n_s, n_d = 16, 8
    up, down = lax.rem(s + 1, n_s), lax.rem(s + n_s - 1, n_s)
    chunk_rows = 256

    cp_grad = pltpu.make_async_copy(grad_h, grad, in_sem.at[0])
    cp_lat = pltpu.make_async_copy(lateral_h, lateral, in_sem.at[1])
    cp_err = pltpu.make_async_copy(error_h, error, in_sem.at[2])
    cp_grad.start()
    cp_lat.start()

    def feats_copy(i):
        rows = pl.ds(pl.multiple_of(i * chunk_rows, chunk_rows), chunk_rows)
        return pltpu.make_async_copy(feats_h.at[rows], feats.at[rows], feats_sem.at[i])

    @pl.loop(0, 8)
    def _(i):
        feats_copy(i).start()

    cp_err.start()

    barrier = pltpu.get_barrier_semaphore()

    @pl.loop(1, n_s)
    def _(i):
        pl.semaphore_signal(barrier, inc=1, device_id={"space": lax.rem(s + i, n_s)}, device_id_type=MESH)

    @pl.loop(1, n_d)
    def _(i):
        pl.semaphore_signal(barrier, inc=1, device_id={"dp": lax.rem(d + i, n_d)}, device_id_type=MESH)

    pl.semaphore_wait(barrier, n_s - 1 + n_d - 1)

    def rim_copy(which, k, side):
        tile = lax.rem(k, 2)
        lanes = pl.ds(pl.multiple_of((k // 2) * 128, 128), 128)
        source, target = (grad_h, halo_g) if which == 0 else (proj, halo_p)
        rows = pl.ds(5, 3) if side == 0 else pl.ds(0, 3)
        at = (which * PIECES + k) * 2 + side
        return pltpu.make_async_remote_copy(
            src_ref=source.at[tile, rows, :, lanes],
            dst_ref=target.at[side, tile, :, :, lanes],
            send_sem=halo_send.at[at],
            recv_sem=halo_recv.at[at],
            device_id={"space": up if side == 0 else down},
            device_id_type=MESH,
        )

    def rim_start(which, k):
        rim_copy(which, k, 0).start()
        rim_copy(which, k, 1).start()

    def rim_wait(which, k):
        rim_copy(which, k, 0).wait()
        rim_copy(which, k, 1).wait()

    for k in range(WINDOW):
        rim_start(0, k)

    row = lax.broadcasted_iota(jnp.int32, (EXT, 128), 0)
    col = lax.broadcasted_iota(jnp.int32, (EXT, 128), 1)
    spread = jnp.where((row % 8) * SEG + row // 8 - HALF == col, 1.0, 0.0).astype(BF)
    row = lax.broadcasted_iota(jnp.int32, (128, 128), 0)
    col = lax.broadcasted_iota(jnp.int32, (128, 128), 1)
    gather = jnp.where((col % 8) * SEG + col // 8 == row, 1.0, 0.0).astype(BF)

    for way in range(2):
        for c in range(TAPS):
            if way == 0:
                taps = [kernel_ref[(6 - a) * 7 + 6 - c : (6 - a) * 7 + 7 - c, :] for a in range(TAPS)]
            else:
                taps = [kernel_ref[a * 7 + c : a * 7 + c + 1, :] for a in range(TAPS)]
            values = leaf_weights(taps + [None])[:LEAVES]
            for leaf, value in enumerate(values):
                weights[way, leaf, c] = jnp.broadcast_to(value, (8, 512))

    cp_lat.wait()

    @pl.loop(0, 8)
    def _(i):
        feats_copy(i).wait()
        rows = pl.ds(pl.multiple_of(i * chunk_rows, chunk_rows), chunk_rows)
        block = jnp.dot(feats[rows, :], lateral[...], preferred_element_type=F32).astype(BF)
        block = block.reshape(2, 128, 512)
        proj[i // 4, pl.ds(lax.rem(i, 4) * 2, 2)] = block

    cp_grad.wait()

    @pl.loop(0, 16)
    def _(i):
        own_g[i] = jnp.dot(spread, grad[i // 8, lax.rem(i, 8)], preferred_element_type=F32)

    def stencil(way, k, halo, own, store):
        tile = lax.rem(k, 2)
        lanes = pl.ds(pl.multiple_of((k // 2) * 128, 128), 128)
        for side in range(2):
            inside = s > 0 if side == 0 else s < n_s - 1
            for i in range(3):
                x = jnp.dot(spread, halo[side, tile, i, :, lanes], preferred_element_type=F32)
                rims[side * 3 + i] = jnp.where(inside, x, 0.0)

        @pl.loop(0, EXT // 16)
        def _(j):
            at = pl.ds(pl.multiple_of(j * 16, 16), 16)
            values = [rims[i, at, :] for i in range(3)]
            values += [own[tile * 8 + i, at, lanes] for i in range(8)]
            values += [rims[3 + i, at, :] for i in range(3)]
            for leaf, value in enumerate(leaf_inputs(values + [None])[:LEAVES]):
                leaf_u[leaf, at, :] = value

        @pl.loop(0, LEAVES // 2)
        def _(pair):
            for leaf in (pair * 2, pair * 2 + 1):
                u = leaf_u[leaf].reshape(SEG + 2 * HALF, 8, 128)
                total = None
                for c in range(TAPS):
                    term = weights[way, leaf, c, :, lanes][None] * u[c : c + SEG]
                    total = term if total is None else total + term
                leaf_v[leaf] = total.reshape(128, 128)

        @pl.loop(0, 8)
        def _(j):
            at = pl.ds(pl.multiple_of(j * 16, 16), 16)
            values = [leaf_v[leaf, at, :] for leaf in range(LEAVES)]
            for i, value in enumerate(leaf_outputs(values + [None])):
                store(tile, lanes, i, at, value.astype(BF))

    def to_pieces(tile, lanes, i, at, value):
        pieces[i, at, :] = value

    def to_sm(tile, lanes, i, at, value):
        sm[tile, i, at, lanes] = value

    @pl.loop(0, PIECES)
    def _(k):
        rim_wait(0, k)

        @pl.when(k + WINDOW < PIECES)
        def _():
            rim_start(0, k + WINDOW)

        @pl.when(k + WINDOW >= PIECES)
        def _():
            rim_start(1, k + WINDOW - PIECES)

        stencil(0, k, halo_g, own_g, to_pieces)
        tile = lax.rem(k, 2)
        lanes = pl.ds(pl.multiple_of((k // 2) * 128, 128), 128)
        for i in range(8):
            gp[tile, i, :, lanes] = jnp.dot(gather, pieces[i], preferred_element_type=F32).astype(BF)

    cp_gp = pltpu.make_async_copy(gp, gp_h, out_sem.at[0])
    cp_gp.start()

    @pl.loop(0, 16)
    def _(i):
        own_p[i] = jnp.dot(spread, proj[i // 8, lax.rem(i, 8)], preferred_element_type=F32)

    q16 = stacked(jnp.transpose(q_ref[...]))
    gq = fold(nt(q16, gp[...].reshape(2048, 512)))
    left = fold(jnp.dot(stacked(gq), feats[...], preferred_element_type=F32))
    cp_err.wait()
    e_high, e_low = split(error[...])
    left = left + fold(nt(q16, e_high)) + fold(nt(q16, e_low))

    def reduce_all(value, blocks, size, buf, rs, part, everyone, out, base):
        buf[...] = jnp.zeros_like(buf)
        for b in range(blocks):
            buf[pl.ds(b, 8, stride=size), :] = value[:, b * 128 : (b + 1) * 128]

        def scatter(i):
            peer = lax.rem(d + i, n_d)
            return pltpu.make_async_remote_copy(
                src_ref=buf.at[pl.ds(pl.multiple_of(peer * size, size), size)],
                dst_ref=rs.at[i - 1],
                send_sem=send1.at[base, i - 1], recv_sem=recv1.at[base, i - 1],
                device_id={"dp": peer}, device_id_type=MESH,
            )

        def across(i):
            return pltpu.make_async_remote_copy(
                src_ref=part, dst_ref=everyone.at[s],
                send_sem=send2.at[base, i - 1], recv_sem=recv2.at[base, i - 1],
                device_id={"space": lax.rem(s + i, n_s)}, device_id_type=MESH,
            )

        mine = pl.ds(pl.multiple_of(d * size, size), size)

        def around(i):
            return pltpu.make_async_remote_copy(
                src_ref=out.at[mine], dst_ref=out.at[mine],
                send_sem=send3.at[base, i - 1], recv_sem=recv3.at[base, i - 1],
                device_id={"dp": lax.rem(d + i, n_d)}, device_id_type=MESH,
            )

        def step1():
            for i in range(1, n_d):
                scatter(i).start()

        def step2():
            for i in range(1, n_d):
                scatter(i).wait()
            total = buf[mine, :]
            for i in range(1, n_d):
                total = total + rs[i - 1]
            part[...] = total
            everyone[s] = total
            for i in range(1, n_s):
                across(i).start()

        def step3():
            for i in range(1, n_s):
                across(i).wait()
            total = everyone[0]
            for i in range(1, n_s):
                total = total + everyone[i]
            out[mine, :] = total * (1.0 / (n_s * n_d))
            for i in range(1, n_d):
                around(i).start()

        def step4():
            for i in range(1, n_d):
                around(i).wait()
            return [out[pl.ds(b, 8, stride=size), :] for b in range(blocks)]

        return step1, step2, step3, step4

    def forward(first, last):
        @pl.loop(first, last)
        def _(k):
            rim_wait(1, k)

            @pl.when(k + WINDOW < PIECES)
            def _():
                rim_start(1, k + WINDOW)

            stencil(1, k, halo_p, own_p, to_sm)

    steps = reduce_all(left, 12, 16, p_buf, p_rs, p_part, p_all, p_out, 0)
    steps[0]()
    forward(0, 1)
    steps[1]()
    forward(1, 2)
    steps[2]()
    forward(2, 3)
    columns = steps[3]()

    at_row = lax.broadcasted_iota(jnp.int32, (8, 128), 0)
    for i in range(8):
        total = None
        lead = [x[i : i + 1, :] for x in columns]
        for x, y in zip(columns, lead):
            total = x * y if total is None else total + x * y
        dots = jnp.sum(total, axis=1, keepdims=True)
        scale = 1.0 / jnp.sqrt(dots[i : i + 1, :] + 1e-06)
        take = jnp.where(at_row[:, :1] > i, dots * scale, 0.0)
        lead = [y * scale for y in lead]
        columns = [jnp.where(at_row == i, y, x - take * y) for x, y in zip(columns, lead)]
    basis = jnp.concatenate(columns, axis=1)
    basis_ref[...] = basis

    b16 = stacked(basis)
    z = fold(nt(b16, feats[...]))
    right = fold(jnp.dot(stacked(z), gp[...].reshape(2048, 512), preferred_element_type=F32))
    e_high, e_low = split(error[...])
    right = right + fold(jnp.dot(b16, e_high, preferred_element_type=F32))
    right = right + fold(jnp.dot(b16, e_low, preferred_element_type=F32))
    steps = reduce_all(right, 4, 8, r_buf, r_rs, r_part, r_all, r_out, 1)
    steps[0]()
    forward(3, 4)
    steps[1]()
    forward(4, 5)
    steps[2]()
    forward(5, 8)
    qt_ref[...] = jnp.concatenate(steps[3](), axis=1)
    cp_sm = pltpu.make_async_copy(sm, sm_h, out_sem.at[1])
    cp_sm.start()
    cp_gp.wait()
    cp_sm.wait()


def final_kernel(feats, gp_all, gp, lateral, sm, error, basis, qt, smoothed, grad_feats, q_next, update, error_next, scratch):
    step = pl.program_id(0)
    grad_feats[...] = nt(gp[...], lateral[...]).astype(BF)
    row = lax.broadcasted_iota(jnp.int32, (128, 128), 0)
    col = lax.broadcasted_iota(jnp.int32, (128, 128), 1)
    gather = jnp.where((col % 8) * SEG + col // 8 == row, 1.0, 0.0).astype(BF)
    for i in range(4):
        smoothed[i] = jnp.dot(gather, sm[i], preferred_element_type=F32).astype(BF)
    tn = (((0,), (0,)), ((), ()))
    b, q = basis[...], qt[...]
    full = lax.dot_general(b, q, tn, precision=lax.Precision.HIGHEST, preferred_element_type=F32)
    matrix = lax.dot_general(feats[...], gp_all[...], tn, preferred_element_type=F32)
    error_next[...] = matrix + error[...] - full
    s = lax.axis_index("space")

    @pl.when(step == s // 4)
    def _():
        scratch[...] = full
        update[...] = scratch[pl.ds(pl.multiple_of(lax.rem(s, 4) * 96, 8), 96), :]

    @pl.when(step == 0)
    def _():
        q_next[...] = jnp.transpose(q)


def body(feats, lateral, kernel, grad_out, error, q_prev):
    flat = feats.reshape(2048, 1536)
    dma = pltpu.SemaphoreType.DMA
    anywhere = pl.BlockSpec(memory_space=pl.ANY)
    vmem = pl.BlockSpec(memory_space=pltpu.VMEM)
    gp, sm, basis, qt = pl.pallas_call(
        main_kernel,
        out_shape=(
            jax.ShapeDtypeStruct((2, 8, 128, 512), BF),
            jax.ShapeDtypeStruct((2, 8, 128, 512), BF),
            jax.ShapeDtypeStruct((8, 1536), F32),
            jax.ShapeDtypeStruct((8, 512), F32),
        ),
        in_specs=[anywhere] * 4 + [vmem] * 2,
        out_specs=(anywhere, anywhere, vmem, vmem),
        scratch_shapes=[
            pltpu.VMEM((2048, 1536), BF),
            pltpu.VMEM((1536, 512), BF),
            pltpu.VMEM((2, 8, 128, 512), BF),
            pltpu.VMEM((1536, 512), F32),
            pltpu.VMEM((2, 8, 128, 512), BF),
            pltpu.VMEM((2, 8, 128, 512), BF),
            pltpu.VMEM((2, 8, 128, 512), BF),
            pltpu.VMEM((2, 2, 3, 128, 512), BF),
            pltpu.VMEM((2, 2, 3, 128, 512), BF),
            pltpu.VMEM((16, EXT, 512), F32),
            pltpu.VMEM((16, EXT, 512), F32),
            pltpu.VMEM((6, EXT, 128), F32),
            pltpu.VMEM((LEAVES, EXT, 128), F32),
            pltpu.VMEM((LEAVES, 128, 128), F32),
            pltpu.VMEM((2, LEAVES, TAPS, 8, 512), F32),
            pltpu.VMEM((8, 128, 128), BF),
            pltpu.VMEM((128, 128), F32),
            pltpu.VMEM((7, 16, 128), F32),
            pltpu.VMEM((16, 128), F32),
            pltpu.VMEM((16, 16, 128), F32),
            pltpu.VMEM((128, 128), F32),
            pltpu.VMEM((64, 128), F32),
            pltpu.VMEM((7, 8, 128), F32),
            pltpu.VMEM((8, 128), F32),
            pltpu.VMEM((16, 8, 128), F32),
            pltpu.VMEM((64, 128), F32),
            dma((3,)),
            dma((8,)),
            dma((2,)),
            dma((32,)),
            dma((32,)),
            dma((2, 7)),
            dma((2, 7)),
            dma((2, 15)),
            dma((2, 15)),
            dma((2, 7)),
            dma((2, 7)),
        ],
        compiler_params=pltpu.CompilerParams(
            collective_id=0, has_side_effects=True, vmem_limit_bytes=60 * 2**20
        ),
        name="exchange",
    )(flat, lateral, grad_out, error, kernel.reshape(49, 512), q_prev)

    rows = gp.reshape(2048, 512)
    whole = lambda *shape: pl.BlockSpec(shape, lambda i: (0,) * len(shape))
    smoothed, grad_feats, q_next, update, error_next = pl.pallas_call(
        final_kernel,
        grid=(4,),
        out_shape=(
            jax.ShapeDtypeStruct((16, 128, 512), BF),
            jax.ShapeDtypeStruct((2048, 1536), BF),
            jax.ShapeDtypeStruct((512, 8), F32),
            jax.ShapeDtypeStruct((96, 512), F32),
            jax.ShapeDtypeStruct((1536, 512), F32),
        ),
        in_specs=[
            pl.BlockSpec((2048, 384), lambda i: (0, i)),
            whole(2048, 512),
            pl.BlockSpec((512, 512), lambda i: (i, 0)),
            whole(1536, 512),
            pl.BlockSpec((4, 128, 512), lambda i: (i, 0, 0)),
            pl.BlockSpec((384, 512), lambda i: (i, 0)),
            pl.BlockSpec((8, 384), lambda i: (0, i)),
            whole(8, 512),
        ],
        out_specs=(
            pl.BlockSpec((4, 128, 512), lambda i: (i, 0, 0)),
            pl.BlockSpec((512, 1536), lambda i: (i, 0)),
            whole(512, 8),
            whole(96, 512),
            pl.BlockSpec((384, 512), lambda i: (i, 0)),
        ),
        scratch_shapes=[pltpu.VMEM((384, 512), F32)],
        compiler_params=pltpu.CompilerParams(vmem_limit_bytes=56 * 2**20),
        name="finish",
    )(flat, rows, rows, lateral, sm.reshape(16, 128, 512), error, basis, qt)
    return (
        smoothed.reshape(2, 8, 128, 512),
        grad_feats.reshape(2, 8, 128, 1536),
        q_next,
        update,
        error_next,
    )


def solution(mesh):
    placed = (
        P("dp", "space", None, None),
        P(),
        P(),
        P("dp", "space", None, None),
        P(("dp", "space"), None),
        P(),
    )
    return jax.shard_map(
        body,
        mesh=mesh,
        in_specs=placed,
        out_specs=(
            P("dp", "space", None, None),
            P("dp", "space", None, None),
            P(),
            P("space", None),
            P(("dp", "space"), None),
        ),
        check_vma=False,
    )
```

time: 373 us -> 94.5 us (0.25)
  other arithmetic: 161 us -> 0 us
  blocking collectives: 135 us -> 0 us
  Pallas kernels: 0 us -> 88.9 us
  matrix products: 31.9 us -> 0 us
  local copies, waits for them, and re-layouts: 26.3 us -> 4.77 us
  starting transfers between devices: 11.5 us -> 0 us
  between operations: 6.24 us -> 0.64 us
    psum x2 -> x0, blocking collectives: 135 us -> none  [the longest x1 71.3 us: combine_columns(): return lax.psum(local_left, ('dp', 'space'))]
    convert_element_type x2 -> x0, other arithmetic: 92 us -> none  [the longest x1 61.2 us: body(): depthwise(jnp.pad(grad_rims, column_pad), kernel, rows, cols, True)]
    pallas_call x0 -> x2, Pallas kernels: none -> 88.9 us  [the longest x1 72 us: body(): pl.pallas_call(main_kernel, out_shape=(jax.ShapeDtypeStruct((2, 8, 128, 5...]
    reduce_sum x14 -> x0, other arithmetic: 39.5 us -> none  [the longest x10 31.2 us: orthonormal(): column = column - jnp.sum(other * column) * other]
    dot_general x6 -> x0, matrix products: 31.9 us -> none  [the longest x1 7.77 us: body(): lax.dot_general(flat, grad_flat, contract, preferred_element_type=jnp.flo...]
    div x4 -> x0, other arithmetic: 17.6 us -> none  [the longest x2 17.6 us: orthonormal(): column = column / jnp.sqrt(jnp.sum(column * column) + 1e-06)]
    ppermute x4 -> x0, starting transfers between devices: 11.5 us -> none  [the longest x2 8.94 us: extended(): lax.ppermute(lax.slice_in_dim(block, block.shape[dim] - width, None, axis...]
    unnamed x22 -> x2, local copies, waits for them, and re-layouts: 14.7 us -> 3.21 us
  transfers between devices with their start and end apart: 4 -> 0, of which waited for: 0 -> 0; matrix products, arithmetic and copies ran while one was open for 49% -> 0% of each run, Pallas kernels for 0% -> 0%
where the time goes in v1:
time: 94.5 us; the launch traced here: 94.3 us
  Pallas kernels  88.9 us (94%)
  local copies, waits for them, and re-layouts  4.77 us (5%)
    pallas_call x1, Pallas kernels, body(): pl.pallas_call(main_kernel, out_shape=(jax.ShapeDtypeStruct((2, 8, 128, 5...  72 us
    pallas_call x1, Pallas kernels, body(): pl.pallas_call(final_kernel, grid=(4,), out_shape=(jax.ShapeDtypeStruct((...  16.8 us
    unnamed x2, local copies, waits for them, and re-layouts  3.21 us

profile of v1, /device:TPU:1, one launch (start us, length us, event | category | flops | bytes accessed | tf_op | source)
XLA Modules:
  0.0 94.3 jit_solution(8410648484147259277)
XLA Ops:
  0.6 1.6 %reshape.29.kernel_ref = f32[49,512]{1,0:T(8,128)} reshape(f32[7,7,512]{2,1,0:T(8,128)} %param.8) | data formatting | bytes 200704 | tf_op jit(solution)/shard_map/reshape | solution.py:441
  2.2 1.6 %copy.11.q_ref = f32[512,8]{1,0:T(8,128)} copy(f32[512,8]{0,1:T(8,128)} %param.11) | data formatting | bytes 32768 | tf_op args[5]
  3.7 72.0 %exchange.1 = (bf16[2,8,128,512]{3,2,1,0:T(8,128)(2,1)}, bf16[2,8,128,512]{3,2,1,0:T(8,128)(2,1)}, f32[8,1536]{1,0:T(8,128)}, f32[8,512]{1,0:T(8,128)}) custom-call(bf16[2048,1536]{1,0:T(8,128)(2,1)} %bitcast.5, bf16[1536,512]{1,0:T(8,128)(2,1)} %lateral.1, bf16[2,8,128,512]{3,2,1,0:T(8,128)(2,1)} %grad_h.1, f32[1536,512]{1,0:T(8,128)} %error.1, ...), custom_call_target="tpu_custom_call" | custom-call | tf_op jit(solution)/shard_map/exchange/pallas_call | solution.py:388
  75.8 16.8 %finish.1 = (bf16[16,128,512]{2,1,0:T(8,128)(2,1)}, bf16[2048,1536]{1,0:T(8,128)(2,1)}, f32[512,8]{1,0:T(8,128)}, f32[96,512]{1,0:T(8,128)}, f32[1536,512]{1,0:T(8,128)}) custom-call(bf16[2048,1536]{1,0:T(8,128)(2,1)} %bitcast.6, bf16[2048,512]{1,0:T(8,128)(2,1)} %bitcast.7, bf16[2048,512]{1,0:T(8,128)(2,1)} %bitcast.8, bf16[1536,512]{1,0:T(8,128)(2,1)} %lateral.1, ...), custom_call_target="tpu_custom_call" | custom-call | tf_op jit(solution)/shard_map/finish/pallas_call | solution.py:445
  92.6 1.7 %copy.12 = f32[512,8]{0,1:T(8,128)} copy(f32[512,8]{1,0:T(8,128)} %get-tuple-element.25) | data formatting | bytes 32768

commit v2 on v1

v2 whole, which is shorter than its diff:
```python
import jax
import jax.numpy as jnp
from jax import lax
from jax.experimental import pallas as pl
from jax.experimental.pallas import tpu as pltpu
from jax.sharding import PartitionSpec as P

MESH = pl.DeviceIdType.MESH
BF = jnp.bfloat16
F32 = jnp.float32
TAPS = 7
HALF = 3
LEAVES = 26
EXT = 144
PIECES = 8
GROUP = 13


def leaf_inputs(d):
    if len(d) == 1:
        return [d[0]]
    size = (len(d) + 1) // 2
    half, span = size // 2, size - 1
    sub = lambda x, y: None if x is None or y is None else x - y
    d0, d1, d2 = d[:span], d[half : half + span], d[size : size + span]
    first = [sub(x, y) for x, y in zip(d0, d1)]
    last = [sub(x, y) for x, y in zip(d2, d1)]
    return leaf_inputs(first) + leaf_inputs(d1) + leaf_inputs(last)


def leaf_weights(h):
    if len(h) == 1:
        return [h[0]]
    half = len(h) // 2
    low, high = h[:half], h[half:]
    both = [x if y is None else x + y for x, y in zip(low, high)]
    return leaf_weights(low) + leaf_weights(both) + leaf_weights(high)


def leaf_outputs(m):
    if len(m) == 1:
        return [m[0]]
    third = len(m) // 3
    first, mid, last = (leaf_outputs(m[i * third : (i + 1) * third]) for i in range(3))
    add = lambda x, y: x if y is None else x + y
    return [add(y, x) for x, y in zip(first, mid)] + [add(x, y) for x, y in zip(mid, last)]


def split(x):
    high = x.astype(BF)
    return high, (x - high.astype(F32)).astype(BF)


def stacked(x):
    high = x.astype(BF).astype(F32)
    return jnp.concatenate([high, x - high], axis=0).astype(BF)


def nt(x, y):
    return lax.dot_general(x, y, (((1,), (1,)), ((), ())), preferred_element_type=F32)


def fold(x):
    return x[:8] + x[8:16]


def main_kernel(
    feats_h, lateral_h, grad_h, error_h, kernel_ref, q_ref,
    gp, sm, matrix, lateral, basis_ref, qt_ref,
    feats, grad, error, proj, halo_g, halo_p, leaf_u, leaf_v, weights, taps_q, spread_q, own_h, far_h,
    p_buf, p_rs, p_part, p_all, p_out, r_buf, r_rs, r_part, r_all, r_out,
    in_sem, feats_sem, halo_send, halo_recv, h_send, h_recv, send1, recv1, send2, recv2, send3, recv3,
):
    s, d = lax.axis_index("space"), lax.axis_index("dp")
    n_s, n_d = 16, 8
    up, down = lax.rem(s + 1, n_s), lax.rem(s + n_s - 1, n_s)
    chunk_rows = 256

    cp_grad = pltpu.make_async_copy(grad_h, grad, in_sem.at[0])
    cp_lat = pltpu.make_async_copy(lateral_h, lateral, in_sem.at[1])
    cp_err = pltpu.make_async_copy(error_h, error, in_sem.at[2])
    cp_grad.start()
    cp_lat.start()

    def feats_copy(i):
        rows = pl.ds(pl.multiple_of(i * chunk_rows, chunk_rows), chunk_rows)
        return pltpu.make_async_copy(feats_h.at[rows], feats.at[rows], feats_sem.at[i])

    @pl.loop(0, 8)
    def _(i):
        feats_copy(i).start()

    cp_err.start()

    barrier = pltpu.get_barrier_semaphore()

    place_x, place_y = s // 4, lax.rem(s, 4)

    def along(axis, i):
        if axis == 0:
            return lax.rem(place_x + i, 4) * 4 + place_y
        return place_x * 4 + lax.rem(place_y + i, 4)

    def greet(**to):
        pl.semaphore_signal(barrier, inc=1, device_id=to, device_id_type=MESH)

    greet(space=up)
    greet(space=down)
    for i in range(1, 4):
        greet(space=along(1, i))
        greet(space=along(0, i))
    for i in range(1, n_d):
        greet(dp=lax.rem(d + i, n_d))
    pl.semaphore_wait(barrier, 2 + 6 + n_d - 1)

    def rim_copy(which, k, side):
        tile = lax.rem(k, 2)
        lanes = pl.ds(pl.multiple_of((k // 2) * 128, 128), 128)
        source, target = (grad_h, halo_g) if which == 0 else (proj, halo_p)
        rows = pl.ds(5, 3) if side == 0 else pl.ds(0, 3)
        at = (which * PIECES + k) * 2 + side
        return pltpu.make_async_remote_copy(
            src_ref=source.at[tile, rows, :, lanes],
            dst_ref=target.at[side, tile, :, :, lanes],
            send_sem=halo_send.at[at],
            recv_sem=halo_recv.at[at],
            device_id={"space": up if side == 0 else down},
            device_id_type=MESH,
        )

    def rim_start(which, k):
        rim_copy(which, k, 0).start()
        rim_copy(which, k, 1).start()

    def rim_wait(which, k):
        rim_copy(which, k, 0).wait()
        rim_copy(which, k, 1).wait()

    def rims_start(which, first, last):
        @pl.loop(first, last)
        def _(k):
            rim_start(which, k)

    rims_start(0, 0, 2)

    for way in range(2):
        for c in range(TAPS):
            if way == 0:
                taps = [kernel_ref[6 - a, 6 - c : 7 - c, :] for a in range(TAPS)]
            else:
                taps = [kernel_ref[a, c : c + 1, :] for a in range(TAPS)]
            values = leaf_weights(taps + [None])[:LEAVES]
            for leaf, value in enumerate(values):
                weights[way, leaf, c] = jnp.broadcast_to(value, (8, 512))

    leaf_u[:, :8, :] = jnp.zeros((LEAVES, 8, 128), F32)
    leaf_u[:, 136:, :] = jnp.zeros((LEAVES, 8, 128), F32)

    q8 = q_ref[...]
    for a in range(TAPS):
        for c in range(TAPS):
            term = kernel_ref[a, c : c + 1, :] * q8
            high = term.astype(BF).astype(F32)
            at = (a * TAPS + c) * 8
            taps_q[0, at : at + 8, :] = high
            taps_q[1, at : at + 8, :] = term - high
    taps_high, taps_low = taps_q[0].astype(BF), taps_q[1].astype(BF)
    cp_grad.wait()
    for i in range(8):
        cells = grad[i // 4, (i % 4) * 2 : (i % 4) * 2 + 2].reshape(256, 512)
        spread_q[:, i * 256 : (i + 1) * 256] = nt(taps_high, cells) + nt(taps_low, cells)
    lane = lax.broadcasted_iota(jnp.int32, (8, 128), 1)

    @pl.loop(0, 2)
    def _(tile):
        for o in range(14):
            total = None
            for c in range(TAPS):
                part = None
                for a in range(max(0, o - 7), min(TAPS, o + 1)):
                    at = (a * TAPS + c) * 8
                    x = spread_q[at : at + 8, pl.ds(pl.multiple_of(tile * 1024 + (o - a) * 128, 128), 128)]
                    part = x if part is None else part + x
                shift = c - HALF
                if shift > 0:
                    part = jnp.where(lane >= shift, pltpu.roll(part, shift, 1), 0.0)
                if shift < 0:
                    part = jnp.where(lane < 128 + shift, pltpu.roll(part, 128 + shift, 1), 0.0)
                total = part if total is None else total + part
            own_h[tile, o] = total

    def h_copy(side):
        return pltpu.make_async_remote_copy(
            src_ref=own_h.at[:, pl.ds(11, 3)] if side == 0 else own_h.at[:, pl.ds(0, 3)],
            dst_ref=far_h.at[side],
            send_sem=h_send.at[side], recv_sem=h_recv.at[side],
            device_id={"space": up if side == 0 else down}, device_id_type=MESH,
        )

    h_copy(0).start()
    h_copy(1).start()
    rims_start(0, 2, 3)

    q16 = stacked(q8)
    cp_err.wait()
    e_high, e_low = split(error[...])
    left = fold(nt(q16, e_high)) + fold(nt(q16, e_low))
    cp_lat.wait()

    def project(first, last):
        @pl.loop(first, last)
        def _(i):
            rows = pl.ds(pl.multiple_of(i * chunk_rows, chunk_rows), chunk_rows)
            block = jnp.dot(feats[rows, :], lateral[...], preferred_element_type=F32).astype(BF)
            proj[i // 4, pl.ds(lax.rem(i, 4) * 2, 2)] = block.reshape(2, 128, 512)

    @pl.loop(0, 8)
    def _(i):
        feats_copy(i).wait()

    def stencil(way, k, halo, own, out):
        tile = lax.rem(k, 2)
        lanes = pl.ds(pl.multiple_of((k // 2) * 128, 128), 128)

        @pl.loop(0, 8, unroll=2)
        def _(j):
            at = pl.ds(pl.multiple_of(j * 16, 16), 16)
            values = [jnp.where(s > 0, halo[0, tile, i, at, lanes].astype(F32), 0.0) for i in range(3)]
            values += [own[tile, i, at, lanes].astype(F32) for i in range(8)]
            values += [jnp.where(s < n_s - 1, halo[1, tile, i, at, lanes].astype(F32), 0.0) for i in range(3)]
            to = pl.ds(pl.multiple_of(j * 16 + 8, 8), 16)
            for leaf, value in enumerate(leaf_inputs(values + [None])[:LEAVES]):
                leaf_u[leaf, to, :] = value

        @pl.loop(0, LEAVES // GROUP)
        def _(group):
            for place in range(GROUP):
                leaf = group * GROUP + place
                taps = [weights[way, leaf, c, :, lanes] for c in range(TAPS)]
                for b in range(16):
                    total = None
                    for c in range(TAPS):
                        term = taps[c] * leaf_u[leaf, pl.ds(8 * b + 8 - HALF + c, 8), :]
                        total = term if total is None else total + term
                    leaf_v[leaf, 8 * b : 8 * b + 8, :] = total

        @pl.loop(0, 8, unroll=2)
        def _(j):
            at = pl.ds(pl.multiple_of(j * 16, 16), 16)
            values = [leaf_v[leaf, at, :] for leaf in range(LEAVES)]
            for i, value in enumerate(leaf_outputs(values + [None])):
                out[tile, i, at, lanes] = value.astype(BF)

    def backward(first, last):
        @pl.loop(first, last)
        def _(k):
            rim_wait(0, k)

            stencil(0, k, halo_g, grad, gp)

    h_copy(0).wait()
    h_copy(1).wait()
    places = []
    for tile in range(2):
        for i in range(8):
            x = own_h[tile, i + HALF]
            if i < HALF:
                x = x + jnp.where(s > 0, far_h[0, tile, i], 0.0)
            if i >= 8 - HALF:
                x = x + jnp.where(s < n_s - 1, far_h[1, tile, i - 8 + HALF], 0.0)
            places.append(x)
    gq = stacked(jnp.concatenate(places, axis=1))
    left = left + fold(jnp.dot(gq, feats[...], preferred_element_type=F32))

    def reduce_all(value, blocks, size, buf, rs, part, lines, out, base):
        buf[...] = jnp.zeros_like(buf)
        for b in range(blocks):
            buf[pl.ds(b, 8, stride=size), :] = value[:, b * 128 : (b + 1) * 128]

        def scatter(i):
            peer = lax.rem(d + i, n_d)
            return pltpu.make_async_remote_copy(
                src_ref=buf.at[pl.ds(pl.multiple_of(peer * size, size), size)],
                dst_ref=rs.at[i - 1],
                send_sem=send1.at[base, i - 1], recv_sem=recv1.at[base, i - 1],
                device_id={"dp": peer}, device_id_type=MESH,
            )

        def across(axis, i):
            at = axis * 3 + i - 1
            return pltpu.make_async_remote_copy(
                src_ref=part.at[axis], dst_ref=lines.at[axis, place_y if axis else place_x],
                send_sem=send2.at[base, at], recv_sem=recv2.at[base, at],
                device_id={"space": along(axis, i)}, device_id_type=MESH,
            )

        def line_start(axis, total):
            part[axis] = total
            lines[axis, place_y if axis else place_x] = total
            for i in range(1, 4):
                across(axis, i).start()

        def line_sum(axis):
            for i in range(1, 4):
                across(axis, i).wait()
            return (lines[axis, 0] + lines[axis, 1]) + (lines[axis, 2] + lines[axis, 3])

        mine = pl.ds(pl.multiple_of(d * size, size), size)

        def around(i):
            return pltpu.make_async_remote_copy(
                src_ref=out.at[mine], dst_ref=out.at[mine],
                send_sem=send3.at[base, i - 1], recv_sem=recv3.at[base, i - 1],
                device_id={"dp": lax.rem(d + i, n_d)}, device_id_type=MESH,
            )

        def step1():
            for i in range(1, n_d):
                scatter(i).start()

        def step2():
            for i in range(1, n_d):
                scatter(i).wait()
            total = buf[mine, :]
            for i in range(1, n_d):
                total = total + rs[i - 1]
            line_start(0, total)

        def step3():
            line_start(1, line_sum(0))

        def step4():
            out[mine, :] = line_sum(1) * (1.0 / (n_s * n_d))
            for i in range(1, n_d):
                around(i).start()

        def step5():
            for i in range(1, n_d):
                around(i).wait()
            return [out[pl.ds(b, 8, stride=size), :] for b in range(blocks)]

        return step1, step2, step3, step4, step5

    def forward(first, last):
        @pl.loop(first, last)
        def _(k):
            rim_wait(1, k)

            stencil(1, k, halo_p, proj, sm)

    steps = reduce_all(left, 12, 16, p_buf, p_rs, p_part, p_all, p_out, 0)
    steps[0]()
    rims_start(0, 3, 4)
    project(0, 4)
    rims_start(0, 4, 5)
    project(4, 8)
    steps[1]()
    rims_start(0, 5, 6)
    backward(0, 2)
    steps[2]()
    rims_start(0, 6, 8)
    backward(2, 5)
    steps[3]()
    rims_start(1, 0, 1)
    backward(5, 7)
    rims_start(1, 1, 2)
    backward(7, 8)
    columns = steps[4]()

    at_row = lax.broadcasted_iota(jnp.int32, (8, 128), 0)
    for i in range(8):
        total = None
        lead = [x[i : i + 1, :] for x in columns]
        for x, y in zip(columns, lead):
            total = x * y if total is None else total + x * y
        dots = jnp.sum(total, axis=1, keepdims=True)
        scale = 1.0 / jnp.sqrt(dots[i : i + 1, :] + 1e-06)
        take = jnp.where(at_row[:, :1] > i, dots * scale, 0.0)
        lead = [y * scale for y in lead]
        columns = [jnp.where(at_row == i, y, x - take * y) for x, y in zip(columns, lead)]
    basis = jnp.concatenate(columns, axis=1)
    basis_ref[...] = basis

    rims_start(1, 2, 3)
    b16 = stacked(basis)
    z = fold(nt(b16, feats[...]))
    right = fold(jnp.dot(stacked(z), gp[...].reshape(2048, 512), preferred_element_type=F32))
    e_high, e_low = split(error[...])
    right = right + fold(jnp.dot(b16, e_high, preferred_element_type=F32))
    right = right + fold(jnp.dot(b16, e_low, preferred_element_type=F32))
    steps = reduce_all(right, 4, 8, r_buf, r_rs, r_part, r_all, r_out, 1)
    steps[0]()

    def gradient(first, last):
        @pl.loop(first, last)
        def _(i):
            at = pl.ds(pl.multiple_of(i * 256, 256), 256)
            tn = (((0,), (0,)), ((), ()))
            block = lax.dot_general(feats[:, at], gp[...].reshape(2048, 512), tn, preferred_element_type=F32)
            matrix[at, :] = block + error[at, :]

    rims_start(1, 3, 4)
    gradient(0, 4)
    forward(0, 1)
    steps[1]()
    rims_start(1, 4, 6)
    forward(1, 3)
    gradient(4, 6)
    steps[2]()
    rims_start(1, 6, 8)
    forward(3, 5)
    steps[3]()
    forward(5, 7)
    qt_ref[...] = jnp.concatenate(steps[4](), axis=1)
    forward(7, 8)


def final_kernel(
    gp, sm, matrix, lateral, basis, qt,
    smoothed, grad_feats, q_next, update, error_next,
    feats_v, error_v, full_v, small_sem, feats_sem, error_sem,
):
    cp_sm = pltpu.make_async_copy(sm, smoothed, small_sem.at[0])
    cp_sm.start()
    b, q = basis[...], qt[...]
    b_high, q_high = b.astype(BF).astype(F32), q.astype(BF).astype(F32)
    b24 = jnp.concatenate([b_high, b - b_high, b_high], axis=0).astype(BF)
    q24 = jnp.concatenate([q_high, q_high, q - q_high], axis=0).astype(BF)
    q_next[...] = q
    s = lax.axis_index("space")
    tn = (((0,), (0,)), ((), ()))

    def feats_copy(i):
        rows = pl.ds(i * 256, 256)
        return pltpu.make_async_copy(feats_v.at[rows], grad_feats.at[rows], feats_sem.at[i])

    def error_copy(i):
        rows = pl.ds(i * 384, 384)
        return pltpu.make_async_copy(error_v.at[rows], error_next.at[rows], error_sem.at[i])

    for i in range(8):
        cells = gp[i // 4, (i % 4) * 2 : (i % 4) * 2 + 2].reshape(256, 512)
        feats_v[i * 256 : (i + 1) * 256, :] = nt(cells, lateral[...]).astype(BF)
        feats_copy(i).start()
        if i % 2 == 0:
            j = i // 2
            full = lax.dot_general(b24[:, j * 384 : (j + 1) * 384], q24, tn, preferred_element_type=F32)
            rows = slice(j * 384, (j + 1) * 384)
            error_v[rows, :] = matrix[rows, :] - full
            error_copy(j).start()

            @pl.when(s // 4 == j)
            def _():
                full_v[...] = full

    update[...] = full_v[pl.ds(pl.multiple_of(lax.rem(s, 4) * 96, 8), 96), :]
    cp_sm.wait()
    for i in range(8):
        feats_copy(i).wait()
    for i in range(4):
        error_copy(i).wait()


def body(feats, lateral, kernel, grad_out, error, q_prev):
    dma = pltpu.SemaphoreType.DMA
    hbm = pl.BlockSpec(memory_space=pltpu.HBM)
    vmem = pl.BlockSpec(memory_space=pltpu.VMEM)
    gp, sm, matrix, weight, basis, qt = pl.pallas_call(
        main_kernel,
        out_shape=(
            pltpu.VMEM((2, 8, 128, 512), BF),
            pltpu.VMEM((2, 8, 128, 512), BF),
            pltpu.VMEM((1536, 512), F32),
            pltpu.VMEM((1536, 512), BF),
            pltpu.VMEM((8, 1536), F32),
            pltpu.VMEM((8, 512), F32),
        ),
        in_specs=[hbm] * 4 + [vmem] * 2,
        out_specs=(vmem,) * 6,
        scratch_shapes=[
            pltpu.VMEM((2048, 1536), BF),
            pltpu.VMEM((2, 8, 128, 512), BF),
            pltpu.VMEM((1536, 512), F32),
            pltpu.VMEM((2, 8, 128, 512), BF),
            pltpu.VMEM((2, 2, 3, 128, 512), BF),
            pltpu.VMEM((2, 2, 3, 128, 512), BF),
            pltpu.VMEM((LEAVES, EXT, 128), F32),
            pltpu.VMEM((LEAVES, 128, 128), F32),
            pltpu.VMEM((2, LEAVES, TAPS, 8, 512), F32),
            pltpu.VMEM((2, 392, 512), F32),
            pltpu.VMEM((392, 2048), F32),
            pltpu.VMEM((2, 14, 8, 128), F32),
            pltpu.VMEM((2, 2, 3, 8, 128), F32),
            pltpu.VMEM((128, 128), F32),
            pltpu.VMEM((7, 16, 128), F32),
            pltpu.VMEM((2, 16, 128), F32),
            pltpu.VMEM((2, 4, 16, 128), F32),
            pltpu.VMEM((128, 128), F32),
            pltpu.VMEM((64, 128), F32),
            pltpu.VMEM((7, 8, 128), F32),
            pltpu.VMEM((2, 8, 128), F32),
            pltpu.VMEM((2, 4, 8, 128), F32),
            pltpu.VMEM((64, 128), F32),
            dma((3,)),
            dma((8,)),
            dma((32,)),
            dma((32,)),
            dma((2,)),
            dma((2,)),
            dma((2, 7)),
            dma((2, 7)),
            dma((2, 6)),
            dma((2, 6)),
            dma((2, 7)),
            dma((2, 7)),
        ],
        compiler_params=pltpu.CompilerParams(
            collective_id=0, has_side_effects=True, vmem_limit_bytes=46 * 2**20
        ),
        name="exchange",
    )(feats.reshape(2048, 1536), lateral, grad_out, error, kernel, q_prev.T)

    smoothed, grad_feats, q_next, update, error_next = pl.pallas_call(
        final_kernel,
        out_shape=(
            jax.ShapeDtypeStruct((2, 8, 128, 512), BF),
            jax.ShapeDtypeStruct((2048, 1536), BF),
            jax.ShapeDtypeStruct((8, 512), F32),
            jax.ShapeDtypeStruct((96, 512), F32),
            jax.ShapeDtypeStruct((1536, 512), F32),
        ),
        in_specs=[vmem] * 6,
        out_specs=(hbm, hbm, vmem, vmem, hbm),
        scratch_shapes=[
            pltpu.VMEM((2048, 1536), BF),
            pltpu.VMEM((1536, 512), F32),
            pltpu.VMEM((384, 512), F32),
            dma((1,)),
            dma((8,)),
            dma((4,)),
        ],
        compiler_params=pltpu.CompilerParams(vmem_limit_bytes=24 * 2**20),
        name="finish",
    )(gp, sm, matrix, weight, basis, qt)
    return smoothed, grad_feats.reshape(2, 8, 128, 1536), q_next.T, update, error_next


def solution(mesh):
    placed = (
        P("dp", "space", None, None),
        P(),
        P(),
        P("dp", "space", None, None),
        P(("dp", "space"), None),
        P(),
    )
    return jax.shard_map(
        body,
        mesh=mesh,
        in_specs=placed,
        out_specs=(
            P("dp", "space", None, None),
            P("dp", "space", None, None),
            P(),
            P("space", None),
            P(("dp", "space"), None),
        ),
        check_vma=False,
    )
```

time: 94.5 us -> 67.1 us (0.71)
  Pallas kernels: 88.9 us -> 66.2 us
  local copies, waits for them, and re-layouts: 4.77 us -> 0 us
    pallas_call x2, Pallas kernels: 88.9 us -> 66.2 us  [the longest x1 59.8 us: body(): pl.pallas_call(main_kernel, out_shape=(pltpu.VMEM((2, 8, 128, 512), BF),...]
    unnamed x2 -> x0, local copies, waits for them, and re-layouts: 3.21 us -> none
    reshape x1 -> x0, local copies, waits for them, and re-layouts: 1.56 us -> none  [body(): kernel.reshape(49, 512)]
where the time goes in v2:
time: 67.1 us; the launch traced here: 67 us
  Pallas kernels  66.2 us (99%)
  between operations  0.8 us (1%)
    pallas_call x1, Pallas kernels, body(): pl.pallas_call(main_kernel, out_shape=(pltpu.VMEM((2, 8, 128, 512), BF),...  59.8 us
    pallas_call x1, Pallas kernels, body(): pl.pallas_call(final_kernel, out_shape=(jax.ShapeDtypeStruct((2, 8, 128,...  6.41 us

profile of v2, /device:TPU:1, one launch (start us, length us, event | category | flops | bytes accessed | tf_op | source)
XLA Modules:
  0.0 67.0 jit_solution(4992854899691510107)
XLA Ops:
  0.6 59.8 %exchange.1 = (bf16[2,8,128,512]{3,2,1,0:T(8,128)(2,1)S(1)}, bf16[2,8,128,512]{3,2,1,0:T(8,128)(2,1)S(1)}, f32[1536,512]{1,0:T(8,128)S(1)}, bf16[1536,512]{1,0:T...) custom-call(bf16[2048,1536]{1,0:T(8,128)(2,1)} %bitcast.4, bf16[1536,512]{1,0:T(8,128)(2,1)} %lateral_h.1, ...), custom_call_target="tpu_custom_call" | custom-call | tf_op jit(solution)/shard_map/exchange/pallas_call | solution.py:468
  60.4 6.4 %finish.1 = (bf16[2,8,128,512]{3,2,1,0:T(8,128)(2,1)}, bf16[2048,1536]{1,0:T(8,128)(2,1)}, f32[8,512]{1,0:T(8,128)}, f32[96,512]{1,0:T(8,128)}, f32[1536,512]{1,0:T(8,128)}) custom-call(bf16[2,8,128,512]{3,2,1,0:T(8,128)(2,1)S(1)} %get-tuple-element.16.gp, bf16[2,8,128,512]{3,2,1,0:T(8,128)(2,1)S(1)} %get-tuple-element.17.sm, ...), custom_call_target="tpu_custom_call" | custom-call | tf_op jit(solution)/shard_map/finish/pallas_call | solution.py:523

commit v3 on v2

--- a/solution.py
+++ b/solution.py
@@ -67,7 +67,7 @@
 def main_kernel(
     feats_h, lateral_h, grad_h, error_h, kernel_ref, q_ref,
     gp, sm, matrix, lateral, basis_ref, qt_ref,
-    feats, grad, error, proj, halo_g, halo_p, leaf_u, leaf_v, weights, taps_q, spread_q, own_h, far_h,
+    error_high, error_low, feats, grad, error, proj, halo_g, halo_p, leaf_u, leaf_v, weights, taps_q, spread_q, own_h, far_h,
     p_buf, p_rs, p_part, p_all, p_out, r_buf, r_rs, r_part, r_all, r_out,
     in_sem, feats_sem, halo_send, halo_recv, h_send, h_recv, send1, recv1, send2, recv2, send3, recv3,
 ):
@@ -111,6 +111,27 @@
         greet(space=along(0, i))
     for i in range(1, n_d):
         greet(dp=lax.rem(d + i, n_d))
+    for way in range(2):
+        for c in range(TAPS):
+            if way == 0:
+                taps = [kernel_ref[6 - a, 6 - c : 7 - c, :] for a in range(TAPS)]
+            else:
+                taps = [kernel_ref[a, c : c + 1, :] for a in range(TAPS)]
+            values = leaf_weights(taps + [None])[:LEAVES]
+            for leaf, value in enumerate(values):
+                weights[way, leaf, c] = jnp.broadcast_to(value, (8, 512))
+
+    leaf_u[:, :8, :] = jnp.zeros((LEAVES, 8, 128), F32)
+    leaf_u[:, 136:, :] = jnp.zeros((LEAVES, 8, 128), F32)
+
+    q8 = q_ref[...]
+    for a in range(TAPS):
+        for c in range(TAPS):
+            term = kernel_ref[a, c : c + 1, :] * q8
+            high = term.astype(BF).astype(F32)
+            at = (a * TAPS + c) * 8
+            taps_q[0, at : at + 8, :] = high
+            taps_q[1, at : at + 8, :] = term - high
     pl.semaphore_wait(barrier, 2 + 6 + n_d - 1)
 
     def rim_copy(which, k, side):
@@ -141,29 +162,8 @@
         def _(k):
             rim_start(which, k)
 
-    rims_start(0, 0, 2)
-
-    for way in range(2):
-        for c in range(TAPS):
-            if way == 0:
-                taps = [kernel_ref[6 - a, 6 - c : 7 - c, :] for a in range(TAPS)]
-            else:
-                taps = [kernel_ref[a, c : c + 1, :] for a in range(TAPS)]
-            values = leaf_weights(taps + [None])[:LEAVES]
-            for leaf, value in enumerate(values):
-                weights[way, leaf, c] = jnp.broadcast_to(value, (8, 512))
-
-    leaf_u[:, :8, :] = jnp.zeros((LEAVES, 8, 128), F32)
-    leaf_u[:, 136:, :] = jnp.zeros((LEAVES, 8, 128), F32)
-
-    q8 = q_ref[...]
-    for a in range(TAPS):
-        for c in range(TAPS):
-            term = kernel_ref[a, c : c + 1, :] * q8
-            high = term.astype(BF).astype(F32)
-            at = (a * TAPS + c) * 8
-            taps_q[0, at : at + 8, :] = high
-            taps_q[1, at : at + 8, :] = term - high
+    rim_start(0, 0)
+
     taps_high, taps_low = taps_q[0].astype(BF), taps_q[1].astype(BF)
     cp_grad.wait()
     for i in range(8):
@@ -199,20 +199,20 @@
 
     h_copy(0).start()
     h_copy(1).start()
-    rims_start(0, 2, 3)
+    rims_start(0, 1, 3)
 
     q16 = stacked(q8)
     cp_err.wait()
-    e_high, e_low = split(error[...])
-    left = fold(nt(q16, e_high)) + fold(nt(q16, e_low))
+    error_high[...], error_low[...] = split(error[...])
+    left = fold(nt(q16, error_high[...])) + fold(nt(q16, error_low[...]))
     cp_lat.wait()
 
     def project(first, last):
         @pl.loop(first, last)
         def _(i):
-            rows = pl.ds(pl.multiple_of(i * chunk_rows, chunk_rows), chunk_rows)
+            rows = pl.ds(pl.multiple_of(i * 1024, 1024), 1024)
             block = jnp.dot(feats[rows, :], lateral[...], preferred_element_type=F32).astype(BF)
-            proj[i // 4, pl.ds(lax.rem(i, 4) * 2, 2)] = block.reshape(2, 128, 512)
+            proj[i] = block.reshape(8, 128, 512)
 
     @pl.loop(0, 8)
     def _(i):
@@ -350,21 +350,19 @@
 
     steps = reduce_all(left, 12, 16, p_buf, p_rs, p_part, p_all, p_out, 0)
     steps[0]()
-    rims_start(0, 3, 4)
-    project(0, 4)
-    rims_start(0, 4, 5)
-    project(4, 8)
+    rims_start(0, 3, 5)
+    project(0, 1)
+    backward(0, 2)
     steps[1]()
     rims_start(0, 5, 6)
-    backward(0, 2)
+    project(1, 2)
+    backward(2, 3)
     steps[2]()
     rims_start(0, 6, 8)
-    backward(2, 5)
+    backward(3, 6)
     steps[3]()
-    rims_start(1, 0, 1)
-    backward(5, 7)
-    rims_start(1, 1, 2)
-    backward(7, 8)
+    rims_start(1, 0, 2)
+    backward(6, 8)
     columns = steps[4]()
 
     at_row = lax.broadcasted_iota(jnp.int32, (8, 128), 0)
@@ -381,38 +379,33 @@
     basis = jnp.concatenate(columns, axis=1)
     basis_ref[...] = basis
 
-    rims_start(1, 2, 3)
+    rims_start(1, 2, 4)
     b16 = stacked(basis)
     z = fold(nt(b16, feats[...]))
     right = fold(jnp.dot(stacked(z), gp[...].reshape(2048, 512), preferred_element_type=F32))
-    e_high, e_low = split(error[...])
-    right = right + fold(jnp.dot(b16, e_high, preferred_element_type=F32))
-    right = right + fold(jnp.dot(b16, e_low, preferred_element_type=F32))
+    right = right + fold(jnp.dot(b16, error_high[...], preferred_element_type=F32))
+    right = right + fold(jnp.dot(b16, error_low[...], preferred_element_type=F32))
     steps = reduce_all(right, 4, 8, r_buf, r_rs, r_part, r_all, r_out, 1)
     steps[0]()
 
     def gradient(first, last):
         @pl.loop(first, last)
         def _(i):
-            at = pl.ds(pl.multiple_of(i * 256, 256), 256)
+            at = pl.ds(pl.multiple_of(i * 768, 768), 768)
             tn = (((0,), (0,)), ((), ()))
             block = lax.dot_general(feats[:, at], gp[...].reshape(2048, 512), tn, preferred_element_type=F32)
             matrix[at, :] = block + error[at, :]
 
-    rims_start(1, 3, 4)
-    gradient(0, 4)
-    forward(0, 1)
+    gradient(0, 2)
     steps[1]()
-    rims_start(1, 4, 6)
-    forward(1, 3)
-    gradient(4, 6)
+    rims_start(1, 4, 5)
+    forward(0, 3)
     steps[2]()
-    rims_start(1, 6, 8)
-    forward(3, 5)
+    rims_start(1, 5, 8)
+    forward(3, 6)
     steps[3]()
-    forward(5, 7)
+    forward(6, 8)
     qt_ref[...] = jnp.concatenate(steps[4](), axis=1)
-    forward(7, 8)
 
 
 def final_kernel(
@@ -431,33 +424,30 @@
     tn = (((0,), (0,)), ((), ()))
 
     def feats_copy(i):
-        rows = pl.ds(i * 256, 256)
+        rows = pl.ds(i * 512, 512)
         return pltpu.make_async_copy(feats_v.at[rows], grad_feats.at[rows], feats_sem.at[i])
 
     def error_copy(i):
         rows = pl.ds(i * 384, 384)
         return pltpu.make_async_copy(error_v.at[rows], error_next.at[rows], error_sem.at[i])
 
-    for i in range(8):
-        cells = gp[i // 4, (i % 4) * 2 : (i % 4) * 2 + 2].reshape(256, 512)
-        feats_v[i * 256 : (i + 1) * 256, :] = nt(cells, lateral[...]).astype(BF)
+    for i in range(4):
+        cells = gp[i // 2, (i % 2) * 4 : (i % 2) * 4 + 4].reshape(512, 512)
+        feats_v[i * 512 : (i + 1) * 512, :] = nt(cells, lateral[...]).astype(BF)
         feats_copy(i).start()
-        if i % 2 == 0:
-            j = i // 2
-            full = lax.dot_general(b24[:, j * 384 : (j + 1) * 384], q24, tn, preferred_element_type=F32)
-            rows = slice(j * 384, (j + 1) * 384)
-            error_v[rows, :] = matrix[rows, :] - full
-            error_copy(j).start()
-
-            @pl.when(s // 4 == j)
-            def _():
-                full_v[...] = full
+        full = lax.dot_general(b24[:, i * 384 : (i + 1) * 384], q24, tn, preferred_element_type=F32)
+        rows = slice(i * 384, (i + 1) * 384)
+        error_v[rows, :] = matrix[rows, :] - full
+        error_copy(i).start()
+
+        @pl.when(s // 4 == i)
+        def _():
+            full_v[...] = full
 
     update[...] = full_v[pl.ds(pl.multiple_of(lax.rem(s, 4) * 96, 8), 96), :]
     cp_sm.wait()
-    for i in range(8):
+    for i in range(4):
         feats_copy(i).wait()
-    for i in range(4):
         error_copy(i).wait()
 
 
@@ -478,6 +468,8 @@
         in_specs=[hbm] * 4 + [vmem] * 2,
         out_specs=(vmem,) * 6,
         scratch_shapes=[
+            pltpu.VMEM((1536, 512), BF),
+            pltpu.VMEM((1536, 512), BF),
             pltpu.VMEM((2048, 1536), BF),
             pltpu.VMEM((2, 8, 128, 512), BF),
             pltpu.VMEM((1536, 512), F32),
@@ -515,7 +507,7 @@
             dma((2, 7)),
         ],
         compiler_params=pltpu.CompilerParams(
-            collective_id=0, has_side_effects=True, vmem_limit_bytes=46 * 2**20
+            collective_id=0, has_side_effects=True, vmem_limit_bytes=48 * 2**20
         ),
         name="exchange",
     )(feats.reshape(2048, 1536), lateral, grad_out, error, kernel, q_prev.T)
@@ -536,7 +528,7 @@
             pltpu.VMEM((1536, 512), F32),
             pltpu.VMEM((384, 512), F32),
             dma((1,)),
-            dma((8,)),
+            dma((4,)),
             dma((4,)),
         ],
         compiler_params=pltpu.CompilerParams(vmem_limit_bytes=24 * 2**20),

time: 67.1 us -> 70.4 us (1.049)
  Pallas kernels: 66.2 us -> 69.3 us
    pallas_call x1, Pallas kernels: 59.8 us -> 62.8 us  [body(): pl.pallas_call(main_kernel, out_shape=(pltpu.VMEM((2, 8, 128, 512), BF),...]
where the time goes in v3:
time: 70.4 us; the launch traced here: 70.2 us
  Pallas kernels  69.3 us (98%)
  between operations  0.8 us (1%)
    pallas_call x1, Pallas kernels, body(): pl.pallas_call(main_kernel, out_shape=(pltpu.VMEM((2, 8, 128, 512), BF),...  62.8 us
    pallas_call x1, Pallas kernels, body(): pl.pallas_call(final_kernel, out_shape=(jax.ShapeDtypeStruct((2, 8, 128,...  6.54 us

profile of v3, /device:TPU:1, one launch (start us, length us, event | category | flops | bytes accessed | tf_op | source)
XLA Modules:
  0.0 70.2 jit_solution(9077868940556612225)
XLA Ops:
  0.6 62.8 %exchange.1 = (bf16[2,8,128,512]{3,2,1,0:T(8,128)(2,1)S(1)}, bf16[2,8,128,512]{3,2,1,0:T(8,128)(2,1)S(1)}, f32[1536,512]{1,0:T(8,128)S(1)}, bf16[1536,512]{1,0:T...) custom-call(bf16[2048,1536]{1,0:T(8,128)(2,1)} %bitcast.4, bf16[1536,512]{1,0:T(8,128)(2,1)} %lateral_h.1, ...), custom_call_target="tpu_custom_call" | custom-call | tf_op jit(solution)/shard_map/exchange/pallas_call | solution.py:458
  63.5 6.5 %finish.1 = (bf16[2,8,128,512]{3,2,1,0:T(8,128)(2,1)}, bf16[2048,1536]{1,0:T(8,128)(2,1)}, f32[8,512]{1,0:T(8,128)}, f32[96,512]{1,0:T(8,128)}, f32[1536,512]{1,0:T(8,128)}) custom-call(bf16[2,8,128,512]{3,2,1,0:T(8,128)(2,1)S(1)} %get-tuple-element.16.gp, bf16[2,8,128,512]{3,2,1,0:T(8,128)(2,1)S(1)} %get-tuple-element.17.sm, ...), custom_call_target="tpu_custom_call" | custom-call | tf_op jit(solution)/shard_map/finish/pallas_call | solution.py:515
